TPU v7x, 256 devices: a whole 4x4x8 slice. The times are simulated.
256 devices in a mesh: dp: 8 (over y, core), seq: 32 (over x, z).
Axes of the slice: x: 4, y: 4, z: 8, core: 2. Of those that a mesh axis runs over, the one named last changes fastest.
Arguments:
- waveform: bfloat16 [8, 1024, 1360], P('dp', 'seq'), may hold values from -6 to 6
- packing: int32 [8, 1024], P(None, 'seq'), may hold values from 0 to 255, as said below
- live_frames: int32 [8, 1024], P('dp', 'seq'), may hold values from 1 to 4
- placing: int32 [8, 1024], P('dp'), may hold values from 0 to 1023, as said below
- first_kernel: bfloat16 [10, 512], replicated, may hold values from -2 to 2
- middle_kernels: bfloat16 [4, 1536, 512], replicated, may hold values from -0.15625 to 0.15625
- last_kernels: bfloat16 [2, 1024, 512], replicated, may hold values from -0.1875 to 0.1875
- norm_gain: float32 [512], replicated, may hold values from 0.1 to 1.9
- norm_bias: float32 [512], replicated, may hold values from -3 to 3
- projection: bfloat16 [512, 1920], replicated, may hold values from -0.25 to 0.25
- projection_bias: float32 [1920], replicated, may hold values from -3 to 3
Outputs:
- encoded: bfloat16 [8, 4096, 1920], P('dp', 'seq')
Inputs may be any that keep to these rules, and one draw needn't show every extreme that they name: For every seq block s, the entries packing[d, s * 32 + k] over all d and k < 32 hold each number below 256 once, and each row d takes exactly 4 of them from each row r (the numbers r * 32 to (r + 1) * 32 - 1). `placing`: each row holds each number below 1024 once; each aligned block of 32 positions takes exactly one number from each aligned block of 32 numbers.
All inputs are finite; a program needn't handle non-finite values.
Results may differ from a plain program's by a relative error of at most 0.02.
Values may be sent and summed in bfloat16 or wider, within the bound.
A program may use at most 128 MiB of HBM per device.

v0:
```python
import jax, jax.numpy as jnp
from jax import lax
from jax.experimental import pallas as pl
from jax.experimental.pallas import tpu as pltpu
BF=jnp.bfloat16; F32=jnp.float32
C=512
NB=32
RG=32

def gelu(z):
    half=z*0.5
    return half*lax.erf(z*0.7071067811865476)+half
def act_rows(h):
    v=jnp.mean(h*h,axis=1,keepdims=True)
    return gelu(h*lax.rsqrt(v+1e-5)).astype(BF)
def center(w):
    w=w.astype(F32)
    return w-jnp.mean(w,axis=1,keepdims=True)

PLAN={0:(271,16),1:(135,15),2:(67,17),3:(33,11),4:(16,8),5:(8,8),6:(4,4)}
def nchunk(l): return -(-PLAN[l][0]//PLAN[l][1])
MAXM=max(v[1] for v in PLAN.values())*NB

def pipeline(n,mm,el,hA,hB):
    mm(0,hA)
    if n==1:
        el(0,hA); return
    def body(j,_):
        mm(2*j+1,hB); el(2*j,hA)
        mm(2*j+2,hA); el(2*j+1,hB)
        return 0
    full=(n-1)//2
    if full>1: lax.fori_loop(0,full,body,0)
    elif full==1: body(0,0)
    if n%2==0:
        mm(n-1,hB); el(n-2,hA); el(n-1,hB)
    else:
        el(n-1,hA)

def build_lhs(xf,lhs):
    for t in range(272):
        o=5*t; j=o//128*128; o-=j
        if o<=118:
            v=xf[:,j:j+128]
            v=pltpu.roll(v,(128-o)%128,1) if o else v
        else:
            v=pltpu.roll(xf[:,j:j+256],256-o,1)[:,:128]
        lhs[t*NB:(t+1)*NB,:]=v.astype(BF)

def extract(xf,w0,wm,wl,lhs,acts,hA,hB):
    build_lhs(xf,lhs)
    for l in range(7):
        T,Tc=PLAN[l]; M=Tc*NB; n=nchunk(l)
        out=acts[l]
        def mm(i,h,l=l,M=M,Tc=Tc):
            if l==0:
                a=lhs[pl.ds(pl.multiple_of(i*M,M),M),:]
                a=jnp.concatenate([a,a],axis=1); w=w0[...]
            else:
                src=acts[l-1]
                s3=src.reshape(src.shape[0]//64,64,C)
                t0=i*Tc
                a=[s3[pl.ds(t0,Tc),0:32,:].reshape(M,C),s3[pl.ds(t0,Tc),32:64,:].reshape(M,C)]
                if l<=4:
                    a.append(s3[pl.ds(t0+1,Tc),0:32,:].reshape(M,C)); w=wm[l-1]
                else: w=wl[l-5]
                a=jnp.concatenate(a,axis=1)
            h[0:M,:]=jnp.dot(a,w,preferred_element_type=F32)
        def el(i,h,l=l,M=M,out=out):
            for r in range(0,M,RG):
                out[pl.ds(pl.multiple_of(i*M,M)+r,RG),:]=act_rows(h[r:r+RG,:])
        pipeline(n,mm,el,hA,hB)

def act_scratch():
    out=[]
    for l in range(7):
        need=nchunk(l)*PLAN[l][1]
        if l<6:
            nxt=nchunk(l+1)*PLAN[l+1][1]
            need=max(need,2*nxt+(2 if l+1<=4 else 0))
        need+=need%2
        out.append(pltpu.VMEM((need*NB,C),BF))
    return out
from jax.sharding import PartitionSpec as P


def kern(x,w0,wm_h,wl_h,gain,bias,o,xf,w0s,wm,wl,lhs,*rest):
    acts=rest[:7]; hA,hB,sem=rest[7:]
    cps=[pltpu.make_async_copy(wm_h,wm,sem.at[0]),pltpu.make_async_copy(wl_h,wl,sem.at[1])]
    for c in cps: c.start()
    xf[:,1280:1536]=jnp.zeros((32,256),F32)
    xf[:,0:1360]=x[...].astype(F32)
    wc=center(w0[...]); hi=wc.astype(BF)
    w0s[...]=jnp.zeros((256,C),BF)
    w0s[0:10,:]=hi; w0s[128:138,:]=(wc-hi.astype(F32)).astype(BF)
    for c in cps: c.wait()
    for l in range(4):
        def b(i,_):
            r=pl.ds(pl.multiple_of(i*128,128),128)
            wm[l,r,:]=center(wm[l,r,:]).astype(BF); return 0
        lax.fori_loop(0,12,b,0)
    for l in range(2):
        def b(i,_):
            r=pl.ds(pl.multiple_of(i*128,128),128)
            wl[l,r,:]=center(wl[l,r,:]).astype(BF); return 0
        lax.fori_loop(0,8,b,0)
    extract(xf,w0s,wm,wl,lhs,acts,hA,hB)
    a=acts[6][0:128,:].astype(F32)
    d=a-jnp.mean(a,axis=1,keepdims=True)
    v=jnp.mean(d*d,axis=1,keepdims=True)
    o[...]=(d*lax.rsqrt(v+1e-5)*gain[...]+bias[...]).astype(BF)
V=pl.BlockSpec(memory_space=pltpu.VMEM); A=pl.BlockSpec(memory_space=pl.ANY)
def call(x,w0,wm,wl,g,b):
    return pl.pallas_call(kern,out_shape=jax.ShapeDtypeStruct((128,C),BF),in_specs=[V,V,A,A,V,V],out_specs=V,
     scratch_shapes=[pltpu.VMEM((32,1536),F32),pltpu.VMEM((256,C),BF),pltpu.VMEM((4,1536,C),BF),pltpu.VMEM((2,1024,C),BF),pltpu.VMEM((272*32,128),BF)]+act_scratch()+[pltpu.VMEM((MAXM,C),F32)]*2+[pltpu.SemaphoreType.DMA((2,))],
     compiler_params=pltpu.CompilerParams(vmem_limit_bytes=60*2**20),name="compute")(x,w0,wm,wl,g,b)


def outgoing(table, owner, per_group):
    groups = table.shape[0]
    portion = per_group // groups
    owned = (table // per_group == owner).astype(jnp.int32)
    ranking = jnp.cumsum(owned, axis=1) - 1
    targets = jnp.arange(portion, dtype=jnp.int32)[None, :, None]
    selected = (owned[:, None, :] == 1) & (ranking[:, None, :] == targets)
    locals_index = jnp.where(selected, (table % per_group)[:, None, :], 0)
    return jnp.sum(locals_index, axis=2).reshape(-1)


def incoming(own_row, per_group, groups):
    portion = per_group // groups
    sources = own_row // per_group
    places = jnp.arange(per_group, dtype=jnp.int32)
    earlier = (sources[:, None] == sources[None, :]) & (places[None, :] <= places[:, None])
    ranking = jnp.sum(earlier.astype(jnp.int32), axis=1) - 1
    return sources * portion + ranking


DEAD = 2.0**100


def body(
    waveform,
    packing,
    live_frames,
    placing,
    first_kernel,
    middle_kernels,
    last_kernels,
    norm_gain,
    norm_bias,
    projection,
    projection_bias,
):
    per_device = waveform.shape[1]
    samples = waveform.shape[2]
    row_count = lax.axis_size("dp")
    shard_count = lax.axis_size("seq")
    dp_index = lax.axis_index("dp")
    seq_index = lax.axis_index("seq")
    own_packing = lax.dynamic_index_in_dim(packing, dp_index, 0, keepdims=False)
    outward = outgoing(packing, dp_index, per_device)
    portion = per_device // row_count
    whole = jnp.concatenate([waveform[0], live_frames[0][:, None].astype(BF)], axis=1)
    send_wave = jnp.take(whole, outward, axis=0).reshape(row_count, portion, samples + 1)
    came_wave = lax.all_to_all(send_wave, "dp", split_axis=0, concat_axis=0, tiled=True)
    inward = incoming(own_packing, per_device, row_count)
    placing_row = placing[0]
    place_table = placing_row.reshape(shard_count, per_device)
    own_places = lax.dynamic_slice_in_dim(placing_row, seq_index * per_device, per_device)
    outward_frames = outgoing(place_table, seq_index, per_device)
    order = jnp.take(inward, outward_frames)
    chosen = jnp.take(came_wave.reshape(-1, samples + 1), order, axis=0)
    ready = call(
        chosen[:, :samples],
        first_kernel,
        middle_kernels,
        last_kernels,
        norm_gain.reshape(1, C),
        norm_bias.reshape(1, C),
    ).reshape(4, NB, C)
    alive = jnp.arange(4)[:, None] < chosen[:, samples].astype(jnp.int32)[None, :]
    ready = jnp.where(alive[:, :, None], ready, jnp.asarray(DEAD, BF))
    came = lax.all_to_all(ready.transpose(1, 0, 2), "seq", split_axis=0, concat_axis=0, tiled=True)
    arrived = jnp.take(came, own_places // per_device, axis=0).reshape(per_device * 4, C)
    projected = (
        jnp.dot(arrived, projection, preferred_element_type=F32) + projection_bias
    )
    dead = arrived[:, :1] > DEAD / 2
    return jnp.where(dead, 0.0, projected).astype(BF)[None]


def solution(mesh):
    placed = (
        P("dp", "seq", None),
        P(None, "seq"),
        P("dp", "seq"),
        P("dp", None),
        P(),
        P(),
        P(),
        P(),
        P(),
        P(),
        P(),
    )
    return jax.shard_map(
        body, mesh=mesh, in_specs=placed, out_specs=P("dp", "seq", None), check_vma=False
    )
```

profile of v0, /device:TPU:1, one launch (start us, length us, event | category | flops | bytes accessed | tf_op | source)
XLA Modules:
  0.0 76.9 jit_solution(16697221368035627240)
XLA Ops:
  0.0 0.0 copy-start
  0.0 0.8 %add_select_fusion.3 = s32[8,32]{1,0:T(8,128)S(1)} fusion(s32[8,32]{1,0:T(8,128)} %param.14), kind=kLoop, calls=%fused_computation.46 | loop fusion | flops 2816 | bytes 2048 | tf_op jit(solution)/shard_map/jit(remainder)/select_n | solution.py:126
  0.8 0.7 broadcast_compare_fusion
  1.5 0.7 convert_bitcast_fusion
  2.2 0.2 reduce_window_sum.22
  2.4 0.1 select_reduce_fusion
  2.5 0.1 copy.18
  2.6 0.1 reshape.342
  2.7 0.7 compare_select_fusion.1
  3.4 0.1 copy.19
  3.5 0.7 compare_and_fusion.1
  4.3 1.0 %pad_maximum_fusion = bf16[32,1361]{1,0:T(8,128)(2,1)S(1)} fusion(bf16[32,1]{1,0:T(8,128)(2,1)S(1)} %copy.19, bf16[32,1360]{1,0:T(8,128)(2,1)} %bitcast.56), kind=kLoop, calls=%fused_computation.11 | loop fusion | flops 174208 | bytes 174208 | tf_op jit(solution)/shard_map/concatenate | solution.py:164
  5.2 0.6 gather_fusion.2
  5.9 0.1 broadcast_select_fusion.2
  6.0 0.7 reshape.343
  6.6 6.5 %all-to-all-start = ((bf16[8,4,1361]{2,1,0:T(4,128)(2,1)}), bf16[8,4,1361]{2,1,0:T(4,128)(2,1)S(1)}, u32[]{:S(2)}, u32[]{:S(2)}) async-start(bf16[8,4,1361]{2,1,0:T(4,128)(2,1)} %reshape.343), calls=%async_computation | async-start | bytes 180224 | tf_op jit(solution)/shard_map/all_to_all | solution.py:166
  13.1 0.7 fusion.22
  13.8 0.6 broadcast.442
  14.4 1.4 %reduce.10 = s32[1024]{0:T(1024)S(1)} reduce(s32[1,1024]{1,0:T(1,128)} %param.16, s32[]{:T(128)} %broadcast.442), dimensions={0}, to_apply=%param.16.reduce_sub_computation.5 | reduce | bytes 8196 | tf_op args[3]
  15.8 0.2 convert_reduce_fusion.1
  16.0 0.1 reshape_squeeze.5
  16.1 0.8 reshape_squeeze.6
  16.9 0.2 reduce_window_sum.23
  17.1 0.1 fusion.8
  17.2 0.7 gather_fusion
  17.9 0.2 all-to-all-done
  18.2 0.6 gather_fusion.3
  18.8 0.1 broadcast_select_fusion.1
  18.9 0.0 copy-start.1
  18.9 0.2 convert_reduce_fusion
  19.1 0.1 iota_compare_fusion.2
  19.2 0.4 copy-done.1
  19.5 0.0 copy-start.2
  19.5 33.9 %compute.1 = bf16[128,512]{1,0:T(8,128)(2,1)} custom-call(bf16[32,1360]{1,0:T(8,128)(2,1)} %bitcast.55, bf16[10,512]{1,0:T(8,128)(2,1)} %w0.1, bf16[4,1536,512]{2,1,0:T(8,128)(2,1)} %wm_h.1, bf16[2,1024,512]{2,1,0:T(8,128)(2,1)} %wl_h.1, f32[1,512]{1,0:T(1,128)} %bitcast.58, f32[1,512]{1,0:T(1,128)} %bitcast.59), custom_call_target="tpu_custom_call" | custom-call | tf_op jit(solution)/shard_map/compute/pallas_call | solution.py:114
  53.4 1.7 %fusion.3 = bf16[32,4,512]{2,1,0:T(4,128)(2,1)} fusion(bf16[4,32,512]{2,1,0:T(8,128)(2,1)} %bitcast.54, pred[4,32]{0,1:T(8,128)(4,1)S(1)} %iota_compare_fusion.2), kind=kLoop, calls=%fused_computation.9 | loop fusion | flops 65536 | bytes 262272 | tf_op jit(solution)/shard_map/transpose | solution.py:184
  55.1 10.5 %all-to-all-start.1 = ((bf16[32,4,512]{2,1,0:T(4,128)(2,1)}), bf16[32,4,512]{2,1,0:T(4,128)(2,1)S(1)}, u32[]{:S(2)}, u32[]{:S(2)}) async-start(bf16[32,4,512]{2,1,0:T(4,128)(2,1)} %fusion.3), calls=%async_computation.1 | async-start | bytes 262144 | tf_op jit(solution)/shard_map/all_to_all | solution.py:184
  65.6 0.1 broadcast_in_dim.87
  65.7 0.1 broadcast_in_dim.88
  65.8 0.7 fusion.21
  66.5 8.2 %all-to-all-done.1 = bf16[32,4,512]{2,1,0:T(4,128)(2,1)S(1)} async-done(((bf16[32,4,512]{2,1,0:T(4,128)(2,1)}), bf16[32,4,512]{2,1,0:T(4,128)(2,1)S(1)}, u32[]{:S(2)}, u32[]{:S(2)}) %all-to-all-start.1) | async-done | bytes 131104 | tf_op jit(solution)/shard_map/all_to_all | solution.py:184
  74.7 0.7 gather_fusion.1
  75.4 0.1 broadcast_select_fusion
  75.5 0.1 compare_reduce_fusion
  75.7 0.0 copy-done
  75.7 0.0 copy-done.2
  75.7 1.2 %fusion.2 = bf16[1,128,1920]{2,1,0:T(8,128)(2,1)} fusion(bf16[128,512]{1,0:T(8,128)(2,1)S(1)} %broadcast_select_fusion, bf16[512,1920]{1,0:T(8,128)(2,1)S(1)} %copy-done, f32[1920]{0:T(1024)S(1)} %copy-done.2, pred[128]{0:T(512)(128)(4,1)S(1)} %compare_reduce_fusion), kind=kOutput, calls=%fused_computation.7 | convolution fusion | flops 252395520 | bytes 2596480 | tf_op jit(solution)/shard_map/dot_general | solution.py:187
  (11 shorter events, 0.2 us)
Async XLA Ops:
  0.0 75.7 %copy-start = (bf16[512,1920]{1,0:T(8,128)(2,1)S(1)}, bf16[512,1920]{1,0:T(8,128)(2,1)}, u32[]{:S(2)}) copy-start(bf16[512,1920]{1,0:T(8,128)(2,1)} %param.22) | copy-start | bytes 5898244
  6.6 11.5 %all-to-all-start = ((bf16[8,4,1361]{2,1,0:T(4,128)(2,1)}), bf16[8,4,1361]{2,1,0:T(4,128)(2,1)S(1)}, u32[]{:S(2)}, u32[]{:S(2)}) async-start(bf16[8,4,1361]{2,1,0:T(4,128)(2,1)} %reshape.343), calls=%async_computation | async-start | bytes 180224 | tf_op jit(solution)/shard_map/all_to_all | solution.py:166
  18.9 0.6 copy-start.1
  19.5 56.2 %copy-start.2 = (f32[1920]{0:T(1024)S(1)}, f32[1920]{0:T(1024)}, u32[]{:S(2)}) copy-start(f32[1920]{0:T(1024)} %param.23) | copy-start | bytes 23044
  55.1 19.6 %all-to-all-start.1 = ((bf16[32,4,512]{2,1,0:T(4,128)(2,1)}), bf16[32,4,512]{2,1,0:T(4,128)(2,1)S(1)}, u32[]{:S(2)}, u32[]{:S(2)}) async-start(bf16[32,4,512]{2,1,0:T(4,128)(2,1)} %fusion.3), calls=%async_computation.1 | async-start | bytes 262144 | tf_op jit(solution)/shard_map/all_to_all | solution.py:184
where the time goes:
time: 78 us; the launch traced here: 76.9 us
  Pallas kernels  33.9 us (43%)
  starting transfers between devices  17 us (22%)
  other arithmetic  10.6 us (14%)
  waiting for transfers between devices  8.38 us (11%)
  local copies, waits for them, and re-layouts  5.64 us (7%)
  matrix products  1.25 us (2%)
    pallas_call x1, Pallas kernels, call(): pl.pallas_call(kern, out_shape=jax.ShapeDtypeStruct((128, C), BF), in_spe...  33.9 us
    all_to_all x1, starting transfers between devices, body(): lax.all_to_all(ready.transpose(1, 0, 2), 'seq', split_axis=0, concat_axis...  10.5 us
    all_to_all x1, waiting for transfers between devices, body(): lax.all_to_all(ready.transpose(1, 0, 2), 'seq', split_axis=0, concat_axis...  8.21 us
    all_to_all x1, starting transfers between devices, body(): lax.all_to_all(send_wave, 'dp', split_axis=0, concat_axis=0, tiled=True)  6.5 us
    transpose x1, other arithmetic, body(): ready.transpose(1, 0, 2)  1.68 us
  transfers between devices with their start and end apart: 2, of which 2 were waited for; matrix products, arithmetic and copies ran while one was open for 7% of the time, Pallas kernels for 0%

commit v1 on v0

v1 whole, which is shorter than its diff:
```python
import jax, jax.numpy as jnp
from jax import lax
from jax.experimental import pallas as pl
from jax.experimental.pallas import tpu as pltpu
BF=jnp.bfloat16; F32=jnp.float32
C=512
NB=32
RG=32

def gelu(z):
    half=z*0.5
    return half*lax.erf(z*0.7071067811865476)+half
def act_rows(h):
    v=jnp.mean(h*h,axis=1,keepdims=True)
    return gelu(h*lax.rsqrt(v+1e-5)).astype(BF)
def center(w):
    w=w.astype(F32)
    return w-jnp.mean(w,axis=1,keepdims=True)

PLAN={0:(271,16),1:(135,15),2:(67,17),3:(33,11),4:(16,8),5:(8,8),6:(4,4)}
def nchunk(l): return -(-PLAN[l][0]//PLAN[l][1])
MAXM=max(v[1] for v in PLAN.values())*NB

def pipeline(n,mm,el,hA,hB):
    mm(0,hA)
    if n==1:
        el(0,hA); return
    def body(j,_):
        mm(2*j+1,hB); el(2*j,hA)
        mm(2*j+2,hA); el(2*j+1,hB)
        return 0
    full=(n-1)//2
    if full>1: lax.fori_loop(0,full,body,0)
    elif full==1: body(0,0)
    if n%2==0:
        mm(n-1,hB); el(n-2,hA); el(n-1,hB)
    else:
        el(n-1,hA)

def build_lhs(xf,lhs):
    for t in range(272):
        o=5*t; j=o//128*128; o-=j
        if o<=118:
            v=xf[:,j:j+128]
            v=pltpu.roll(v,(128-o)%128,1) if o else v
        else:
            v=pltpu.roll(xf[:,j:j+256],256-o,1)[:,:128]
        lhs[t*NB:(t+1)*NB,:]=v.astype(BF)

def extract(xf,w0,wm,wl,lhs,acts,hA,hB):
    build_lhs(xf,lhs)
    for l in range(7):
        T,Tc=PLAN[l]; M=Tc*NB; n=nchunk(l)
        out=acts[l]
        def mm(i,h,l=l,M=M,Tc=Tc):
            if l==0:
                a=lhs[pl.ds(pl.multiple_of(i*M,M),M),:]
                a=jnp.concatenate([a,a],axis=1); w=w0[...]
            else:
                src=acts[l-1]
                s3=src.reshape(src.shape[0]//64,64,C)
                t0=i*Tc
                a=[s3[pl.ds(t0,Tc),0:32,:].reshape(M,C),s3[pl.ds(t0,Tc),32:64,:].reshape(M,C)]
                if l<=4:
                    a.append(s3[pl.ds(t0+1,Tc),0:32,:].reshape(M,C)); w=wm[l-1]
                else: w=wl[l-5]
                a=jnp.concatenate(a,axis=1)
            h[0:M,:]=jnp.dot(a,w,preferred_element_type=F32)
        def el(i,h,l=l,M=M,out=out):
            base=pl.multiple_of(i*M,M)
            def rows(r,_):
                out[pl.ds(base+r*RG,RG),:]=act_rows(h[pl.ds(r*RG,RG),:])
                return 0
            lax.fori_loop(0,M//RG,rows,0,unroll=True)
        pipeline(n,mm,el,hA,hB)

def act_scratch():
    out=[]
    for l in range(7):
        need=nchunk(l)*PLAN[l][1]
        if l<6:
            nxt=nchunk(l+1)*PLAN[l+1][1]
            need=max(need,2*nxt+(2 if l+1<=4 else 0))
        need+=need%2
        out.append(pltpu.VMEM((need*NB,C),BF))
    return out
from jax.sharding import PartitionSpec as P


MESH=pl.DeviceIdType.MESH
I32=jnp.int32
ROWS=8
SHARDS=32
TILES=11
SLAB=48
SAMPLES=1360
DEAD=2.0**100

def iota(shape,dim): return lax.broadcasted_iota(I32,shape,dim)
def earlier_counts(owned):
    tri=(iota((NB,NB),0)<iota((NB,NB),1)).astype(F32).astype(BF)
    return jnp.dot(owned.astype(F32).astype(BF),tri,preferred_element_type=F32)

def dp_peer(k):
    return lax.rem(lax.axis_index("dp")+k,ROWS)
def seq_peer(k):
    return lax.rem(lax.axis_index("seq")+k,SHARDS)
def row_of_shard(s):
    return lax.rem(s,4)*8+s//4

def greet():
    barrier=pltpu.get_barrier_semaphore()
    def a(k,_):
        pl.semaphore_signal(barrier,inc=1,device_id={"dp":dp_peer(k)},device_id_type=MESH); return 0
    lax.fori_loop(1,ROWS,a,0)
    def b(k,_):
        pl.semaphore_signal(barrier,inc=1,device_id={"seq":seq_peer(k)},device_id_type=MESH); return 0
    lax.fori_loop(1,SHARDS,b,0)
    return barrier

def pack_waves(wave,packing,live,xa,tall,send):
    me=lax.axis_index("dp")
    xa[:,1280:1408]=jnp.zeros((NB,128),BF)
    xa[:,0:SAMPLES]=wave[...]
    table=packing[...]
    owned=(table>>5)==me
    count=earlier_counts(owned)
    parts=[]
    for i in range(4):
        chosen=owned&(count==float(i))
        index=jnp.sum(jnp.where(chosen,table&31,0),axis=1,keepdims=True)
        parts.append(jnp.where(iota((8,NB),1)==index,1.0,0.0))
    pick=jnp.concatenate(parts,axis=0)
    lives=jnp.sum(pick*live[...].astype(F32),axis=1,keepdims=True)
    pick=pick.astype(BF)
    y=jnp.dot(pick,xa[...],preferred_element_type=F32)
    for j in range(TILES):
        tile=y[:,j*128:(j+1)*128]
        if j==TILES-1:
            tile=jnp.where(iota((NB,128),1)==SAMPLES-1280,lives,tile)
        for i in range(4):
            tall[pl.ds(i*TILES+j,8,stride=SLAB),:]=tile[i*8:(i+1)*8,:]
    for d in range(ROWS):
        send[d]=tall[d*SLAB:(d+1)*SLAB,:].astype(BF)

def wave_copy(k,send,recv,ssem,rsem):
    return pltpu.make_async_remote_copy(src_ref=send.at[dp_peer(k)],dst_ref=recv.at[lax.axis_index("dp")],
        send_sem=ssem.at[k],recv_sem=rsem.at[k],device_id={"dp":dp_peer(k)},device_id_type=MESH)
def frame_copy(k,send,recv,ssem,rsem):
    return pltpu.make_async_remote_copy(src_ref=send.at[row_of_shard(seq_peer(k))],dst_ref=recv.at[lax.axis_index("seq")],
        send_sem=ssem.at[k],recv_sem=rsem.at[k],device_id={"seq":seq_peer(k)},device_id_type=MESH)

def order_rows(packing,placing):
    me_d,me_s=lax.axis_index("dp"),lax.axis_index("seq")
    own=packing[pl.ds(me_d,1),:]
    owned=(own>>5)==iota((ROWS,NB),0)
    count=earlier_counts(owned)
    slots=jnp.concatenate([jnp.where(owned&(count==float(i)),1.0,0.0) for i in range(4)],axis=0)
    table=placing[...]
    parts=[]
    for g in range(4):
        mine=((table>>5)==me_s)&((iota((8,128),1)>>5)==g)
        index=jnp.sum(jnp.where(mine,table&31,0),axis=1,keepdims=True)
        parts.append(jnp.where(iota((8,NB),1)==index,1.0,0.0))
    taken=jnp.concatenate(parts,axis=0)
    return lax.dot_general(taken.astype(BF),slots.astype(BF),(((1,),(1,)),((),())),preferred_element_type=F32).astype(BF)

def unpack_waves(recv,order,tall,xa,xf):
    for r in range(ROWS):
        tall[r*SLAB:(r+1)*SLAB,:]=recv[r].astype(F32)
    for j in range(TILES):
        tile=jnp.concatenate([tall[pl.ds(i*TILES+j,8,stride=SLAB),:] for i in range(4)],axis=0)
        xa[:,j*128:(j+1)*128]=tile.astype(BF)
    xf[:,0:1408]=jnp.dot(order,xa[...],preferred_element_type=F32)
    xf[:,1408:1536]=jnp.zeros((NB,128),F32)

def frame_order(placing):
    me=lax.axis_index("seq")
    row=placing[pl.ds(me//4,1),:]
    at=lax.rem(me,4)*32
    shape=(128,128)
    hit=iota(shape,1)==at+(iota(shape,0)>>2)
    source=jnp.sum(jnp.where(hit,row>>5,0),axis=1,keepdims=True)
    return jnp.where(iota(shape,1)==source*4+(iota(shape,0)&3),1.0,0.0).astype(BF)

def pack_frames(act,lives,gain,bias,tall,send):
    for f in range(4):
        a=act[f*NB:(f+1)*NB,:].astype(F32)
        d=a-jnp.mean(a,axis=1,keepdims=True)
        v=jnp.mean(d*d,axis=1,keepdims=True)
        ready=d*lax.rsqrt(v+1e-5)*gain[...]+bias[...]
        ready=jnp.where(lives>f+0.5,ready,DEAD)
        for j in range(4):
            tall[pl.ds(f*4+j,NB,stride=16),:]=ready[:,j*128:(j+1)*128]
    for b in range(NB):
        send[b]=tall[b*16:(b+1)*16,:].astype(BF)

def unpack_frames(recv,order,tall,out):
    for s in range(SHARDS):
        tall[s*16:(s+1)*16,:]=recv[s].astype(F32)
    a=jnp.concatenate([tall[pl.ds(j,128,stride=4),:] for j in range(4)],axis=1).astype(BF)
    out[...]=jnp.dot(order,a,preferred_element_type=F32).astype(BF)

def center_all(ref,depth):
    for l in range(ref.shape[0]):
        def b(i,_):
            r=pl.ds(pl.multiple_of(i*128,128),128)
            ref[l,r,:]=center(ref[l,r,:]).astype(BF); return 0
        lax.fori_loop(0,depth//128,b,0)

def mega(wave,packing,live,placing,w0,wm_h,wl_h,gain,bias,out,
         xf,w0s,wm,wl,lhs,*rest):
    acts=rest[:7]
    hA,hB,xa,tall,tall2,send1,recv1,send2,recv2,wsem,s1,r1,s2,r2=rest[7:]
    cps=[pltpu.make_async_copy(wm_h.at[l],wm.at[l],wsem.at[l]) for l in range(4)]
    cps+=[pltpu.make_async_copy(wl_h.at[l],wl.at[l],wsem.at[4+l]) for l in range(2)]
    for c in cps: c.start()
    barrier=greet()
    pack_waves(wave,packing,live,xa,tall,send1)
    pl.semaphore_wait(barrier,ROWS-1+SHARDS-1)
    def go(k,_):
        wave_copy(k,send1,recv1,s1,r1).start(); return 0
    lax.fori_loop(1,ROWS,go,0)
    me=lax.axis_index("dp")
    recv1[me]=send1[me]
    order=order_rows(packing,placing)
    forder=frame_order(placing)
    wc=center(w0[...]); hi=wc.astype(BF)
    w0s[...]=jnp.zeros((256,C),BF)
    w0s[0:10,:]=hi; w0s[128:138,:]=(wc-hi.astype(F32)).astype(BF)
    for c in cps: c.wait()
    center_all(wm,1536); center_all(wl,1024)
    def done(k,_):
        wave_copy(k,send1,recv1,s1,r1).wait(); return 0
    lax.fori_loop(1,ROWS,done,0)
    unpack_waves(recv1,order,tall,xa,xf)
    extract(xf,w0s,wm,wl,lhs,acts,hA,hB)
    lives=jnp.sum(jnp.where(iota((NB,128),1)==SAMPLES-1280,xf[:,1280:1408],0.0),axis=1,keepdims=True)
    pack_frames(acts[6],lives,gain,bias,tall2,send2)
    def go2(k,_):
        frame_copy(k,send2,recv2,s2,r2).start(); return 0
    lax.fori_loop(1,SHARDS,go2,0)
    ms=lax.axis_index("seq")
    recv2[ms]=send2[row_of_shard(ms)]
    def done2(k,_):
        frame_copy(k,send2,recv2,s2,r2).wait(); return 0
    lax.fori_loop(1,SHARDS,done2,0)
    unpack_frames(recv2,forder,tall2,out)

def call_mega(wave,packing,live,placing,w0,wm,wl,g,b):
    V=pl.BlockSpec(memory_space=pltpu.VMEM); A=pl.BlockSpec(memory_space=pl.ANY)
    D=pltpu.SemaphoreType.DMA
    return pl.pallas_call(mega,out_shape=jax.ShapeDtypeStruct((128,C),BF),
     in_specs=[V,V,V,V,V,A,A,V,V],out_specs=V,
     scratch_shapes=[pltpu.VMEM((32,1536),F32),pltpu.VMEM((256,C),BF),pltpu.VMEM((4,1536,C),BF),pltpu.VMEM((2,1024,C),BF),
       pltpu.VMEM((272*32,128),BF)]+act_scratch()+[pltpu.VMEM((MAXM,C),F32)]*2+[
       pltpu.VMEM((NB,1408),BF),pltpu.VMEM((ROWS*SLAB,128),F32),pltpu.VMEM((SHARDS*16,128),F32),
       pltpu.VMEM((ROWS,SLAB,128),BF),pltpu.VMEM((ROWS,SLAB,128),BF),pltpu.VMEM((SHARDS,16,128),BF),pltpu.VMEM((SHARDS,16,128),BF),
       D((6,)),D((ROWS,)),D((ROWS,)),D((SHARDS,)),D((SHARDS,))],
     compiler_params=pltpu.CompilerParams(vmem_limit_bytes=60*2**20,collective_id=0,has_side_effects=True),name="extract")(
       wave,packing,live,placing,w0,wm,wl,g,b)


def body(
    waveform,
    packing,
    live_frames,
    placing,
    first_kernel,
    middle_kernels,
    last_kernels,
    norm_gain,
    norm_bias,
    projection,
    projection_bias,
):
    arrived = call_mega(
        waveform[0],
        packing,
        live_frames,
        placing.reshape(8, 128),
        first_kernel,
        middle_kernels,
        last_kernels,
        norm_gain.reshape(1, C),
        norm_bias.reshape(1, C),
    )
    projected = (
        jnp.dot(arrived, projection, preferred_element_type=F32) + projection_bias
    )
    dead = arrived[:, :1] > DEAD / 2
    return jnp.where(dead, 0.0, projected).astype(BF)[None]


def solution(mesh):
    placed = (
        P("dp", "seq", None),
        P(None, "seq"),
        P("dp", "seq"),
        P("dp", None),
        P(),
        P(),
        P(),
        P(),
        P(),
        P(),
        P(),
    )
    return jax.shard_map(
        body, mesh=mesh, in_specs=placed, out_specs=P("dp", "seq", None), check_vma=False
    )
```

time: 78 us -> 50.6 us (0.65); the launches traced: 76.9 us -> 50.4 us
  starting transfers between devices: 17 us -> 0 us
  Pallas kernels: 33.9 us -> 47.3 us
  other arithmetic: 10.6 us -> 0.86 us
  waiting for transfers between devices: 8.38 us -> 0 us
  local copies, waits for them, and re-layouts: 5.64 us -> 0.01 us
  matrix products: 1.25 us -> 2.15 us
    all_to_all x2 -> x0, starting transfers between devices: 17 us -> none  [the longest x1 10.5 us: body(): lax.all_to_all(ready.transpose(1, 0, 2), 'seq', split_axis=0, concat_axis...]
    pallas_call x1, Pallas kernels: 33.9 us -> 47.3 us  [call_mega(): pl.pallas_call(mega, out_shape=jax.ShapeDtypeStruct((128, C), BF), in_spe...]
    all_to_all x2 -> x0, waiting for transfers between devices: 8.38 us -> none  [the longest x1 8.21 us: body(): lax.all_to_all(ready.transpose(1, 0, 2), 'seq', split_axis=0, concat_axis...]
    gather x5 -> x0, local copies, waits for them, and re-layouts: 2.69 us -> none  [the longest x2 0.71 us: body(): jnp.take(came, own_places // per_device, axis=0).reshape(per_device * 4, C)]
    select_n x7 -> x0, other arithmetic: 2.55 us -> none  [the longest x1 0.84 us: outgoing(): locals_index = jnp.where(selected, (table % per_group)[:, None, :], 0)]
    transpose x1 -> x0, other arithmetic: 1.68 us -> none  [body(): ready.transpose(1, 0, 2)]
    eq x2 -> x0, other arithmetic: 1.4 us -> none  [the longest x1 0.7 us: outgoing(): selected = (owned[:, None, :] == 1) & (ranking[:, None, :] == targets)]
    unnamed x1 -> x0, other arithmetic: 1.39 us -> none
  transfers between devices with their start and end apart: 2 -> 0, of which waited for: 2 -> 0; matrix products, arithmetic and copies ran while one was open for 7% -> 0% of each run, Pallas kernels for 0% -> 0%
where the time goes in v1:
time: 50.6 us; the launch traced here: 50.4 us
  Pallas kernels  47.3 us (93%)
  matrix products  2.15 us (4%)
  other arithmetic  0.86 us (2%)
    pallas_call x1, Pallas kernels, call_mega(): pl.pallas_call(mega, out_shape=jax.ShapeDtypeStruct((128, C), BF), in_spe...  47.3 us
    dot_general x1, matrix products, body(): jnp.dot(arrived, projection, preferred_element_type=F32) + projection_bias  2.15 us

profile of v1, /device:TPU:1, one launch (start us, length us, event | category | flops | bytes accessed | tf_op | source)
XLA Modules:
  0.0 50.4 jit_solution(15733825550900731862)
XLA Ops:
  0.0 0.0 copy-start
  0.0 0.0 copy-start.1
  0.0 47.3 %extract.1 = bf16[128,512]{1,0:T(8,128)(2,1)} custom-call(bf16[32,1360]{1,0:T(8,128)(2,1)} %bitcast.8, s32[8,32]{1,0:T(8,128)} %packing.1, s32[1,32]{1,0:T(1,128)} %live.1, s32[8,128]{1,0:T(8,128)} %bitcast.9, bf16[10,512]{1,0:T(8,128)(2,1)} %w0.1, bf16[4,1536,512]{2,1,0:T(8,128)(2,1)} %wm_h.1, bf16[2,1024,512]{2,1,0:T(8,128)(2,1)} %wl_h.1, ...), custom_call_target="tpu_custom_call" | custom-call | tf_op jit(solution)/shard_map/extract/pallas_call | solution.py:253
  47.4 0.9 %compare_reduce_fusion = pred[128]{0:T(512)(128)(4,1)S(1)} fusion(bf16[128,512]{1,0:T(8,128)(2,1)} %extract.1), kind=kLoop, calls=%fused_computation.4 | loop fusion | flops 128 | bytes 384 | tf_op jit(solution)/shard_map/gt | solution.py:291
  48.2 0.0 copy-done
  48.2 0.0 copy-done.1
  48.2 2.1 %fusion.2 = bf16[1,128,1920]{2,1,0:T(8,128)(2,1)} fusion(bf16[128,512]{1,0:T(8,128)(2,1)} %extract.1, bf16[512,1920]{1,0:T(8,128)(2,1)S(1)} %copy-done, f32[1920]{0:T(1024)S(1)} %copy-done.1, pred[128]{0:T(512)(128)(4,1)S(1)} %compare_reduce_fusion), kind=kOutput, calls=%fused_computation.3 | convolution fusion | flops 252395520 | bytes 2596480 | tf_op jit(solution)/shard_map/dot_general | solution.py:289
Async XLA Ops:
  0.0 48.2 %copy-start = (bf16[512,1920]{1,0:T(8,128)(2,1)S(1)}, bf16[512,1920]{1,0:T(8,128)(2,1)}, u32[]{:S(2)}) copy-start(bf16[512,1920]{1,0:T(8,128)(2,1)} %param.20) | copy-start | bytes 5898244
  0.0 48.2 %copy-start.1 = (f32[1920]{0:T(1024)S(1)}, f32[1920]{0:T(1024)}, u32[]{:S(2)}) copy-start(f32[1920]{0:T(1024)} %param.21) | copy-start | bytes 23044

commit v2 on v1

--- a/solution.py
+++ b/solution.py
@@ -7,19 +7,20 @@
 NB=32
 RG=32
 
-def gelu(z):
-    half=z*0.5
-    return half*lax.erf(z*0.7071067811865476)+half
-def act_rows(h):
-    v=jnp.mean(h*h,axis=1,keepdims=True)
-    return gelu(h*lax.rsqrt(v+1e-5)).astype(BF)
+def act_rows(h,eps):
+    total=jnp.sum(h*h,axis=1,keepdims=True)
+    y=h*lax.rsqrt(total*(2.0/C)+2.0*eps)
+    return (y*lax.erf(y)+y).astype(BF)
 def center(w):
     w=w.astype(F32)
     return w-jnp.mean(w,axis=1,keepdims=True)
 
-PLAN={0:(271,16),1:(135,15),2:(67,17),3:(33,11),4:(16,8),5:(8,8),6:(4,4)}
+F1=8
+EPS=1e-05
+PLAN={0:(272,16),1:(136,8),2:(67,17),3:(33,11),4:(16,8),5:(8,8),6:(4,4)}
 def nchunk(l): return -(-PLAN[l][0]//PLAN[l][1])
-MAXM=max(v[1] for v in PLAN.values())*NB
+HM=max(max(v[1] for v in PLAN.values())*NB,2*F1*NB)
+GM=F1*NB
 
 def pipeline(n,mm,el,hA,hB):
     mm(0,hA)
@@ -47,43 +48,70 @@
             v=pltpu.roll(xf[:,j:j+256],256-o,1)[:,:128]
         lhs[t*NB:(t+1)*NB,:]=v.astype(BF)
 
-def extract(xf,w0,wm,wl,lhs,acts,hA,hB):
+def first_two(lhs,w0,w1,pair,act1,hs,gs):
+    n=136//F1; M1=F1*NB; M0=2*M1; E=2*NB
+    def mm0(i,h):
+        a=lhs[pl.ds(pl.multiple_of(i*M0,M0),M0),:]
+        h[0:M0,:]=jnp.dot(jnp.concatenate([a,a],axis=1),w0[...],preferred_element_type=F32)
+    def mm1(g,src):
+        v=src.reshape(F1+1,2*NB,C)
+        a=jnp.concatenate([v[0:F1,0:NB,:].reshape(M1,C),v[0:F1,NB:2*NB,:].reshape(M1,C),
+            v[1:F1+1,0:NB,:].reshape(M1,C)],axis=1)
+        g[0:M1,:]=jnp.dot(a,w1[...],preferred_element_type=F32)
+    def el0(h,out,nxt):
+        for r in range(0,M0,RG):
+            v=act_rows(h[r:r+RG,:],EPS)
+            out[E+r:E+r+RG,:]=v
+            if r>=M0-E: nxt[r-(M0-E):r-(M0-E)+RG,:]=v
+    def el1(i,g):
+        base=pl.multiple_of(i*M1,M1)
+        for r in range(0,M1,RG):
+            act1[pl.ds(base+r,RG),:]=act_rows(g[r:r+RG,:],2*EPS)
+    def step(i,par,m0=True,e0=True,m1=True,e1=True):
+        if m0: mm0(i+1,hs[1-par])
+        if m1: mm1(gs[1-par],pair[1-par])
+        if e0: el0(hs[par],pair[par],pair[1-par])
+        if e1: el1(i-2,gs[par])
+    mm0(0,hs[0])
+    step(0,0,m1=False,e1=False)
+    step(1,1,e1=False)
+    pairs=(n-3)//2
+    def body(j,_):
+        step(2+2*j,0); step(3+2*j,1)
+        return 0
+    lax.fori_loop(0,pairs,body,0)
+    for i in range(2+2*pairs,n+2):
+        step(i,i%2,m0=i+1<n,e0=i<n,m1=0<=i-1<n,e1=0<=i-2<n)
+
+def extract(xf,w0,wm,wl,lhs,acts,hA,hB,gA,gB):
     build_lhs(xf,lhs)
-    for l in range(7):
+    first_two(lhs,w0,wm.at[0],acts[0:2],acts[2],(hA,hB),(gA,gB))
+    for l in range(2,7):
         T,Tc=PLAN[l]; M=Tc*NB; n=nchunk(l)
-        out=acts[l]
+        out=acts[l+1]
         def mm(i,h,l=l,M=M,Tc=Tc):
-            if l==0:
-                a=lhs[pl.ds(pl.multiple_of(i*M,M),M),:]
-                a=jnp.concatenate([a,a],axis=1); w=w0[...]
+            src=acts[l]
+            s3=src.reshape(src.shape[0]//64,64,C)
+            t0=i*Tc
+            if l==2:
+                a=[s3[pl.ds(t0,Tc),32:64,:],s3[pl.ds(t0+1,Tc),0:32,:],s3[pl.ds(t0+1,Tc),32:64,:]]
             else:
-                src=acts[l-1]
-                s3=src.reshape(src.shape[0]//64,64,C)
-                t0=i*Tc
-                a=[s3[pl.ds(t0,Tc),0:32,:].reshape(M,C),s3[pl.ds(t0,Tc),32:64,:].reshape(M,C)]
-                if l<=4:
-                    a.append(s3[pl.ds(t0+1,Tc),0:32,:].reshape(M,C)); w=wm[l-1]
-                else: w=wl[l-5]
-                a=jnp.concatenate(a,axis=1)
-            h[0:M,:]=jnp.dot(a,w,preferred_element_type=F32)
+                a=[s3[pl.ds(t0,Tc),0:32,:],s3[pl.ds(t0,Tc),32:64,:]]
+                if l<=4: a.append(s3[pl.ds(t0+1,Tc),0:32,:])
+            a=[v.reshape(M,C) for v in a]
+            w=wm[l-1] if l<=4 else wl[l-5]
+            h[0:M,:]=jnp.dot(jnp.concatenate(a,axis=1),w,preferred_element_type=F32)
         def el(i,h,l=l,M=M,out=out):
             base=pl.multiple_of(i*M,M)
             def rows(r,_):
-                out[pl.ds(base+r*RG,RG),:]=act_rows(h[pl.ds(r*RG,RG),:])
+                out[pl.ds(base+r*RG,RG),:]=act_rows(h[pl.ds(r*RG,RG),:],2*EPS)
                 return 0
             lax.fori_loop(0,M//RG,rows,0,unroll=True)
         pipeline(n,mm,el,hA,hB)
 
 def act_scratch():
-    out=[]
-    for l in range(7):
-        need=nchunk(l)*PLAN[l][1]
-        if l<6:
-            nxt=nchunk(l+1)*PLAN[l+1][1]
-            need=max(need,2*nxt+(2 if l+1<=4 else 0))
-        need+=need%2
-        out.append(pltpu.VMEM((need*NB,C),BF))
-    return out
+    frames=[2*F1+2,2*F1+2,138,68,34,16,8,4]
+    return [pltpu.VMEM((f*NB,C),BF) for f in frames]
 from jax.sharding import PartitionSpec as P
 
 
@@ -94,6 +122,7 @@
 TILES=11
 SLAB=48
 SAMPLES=1360
+WIDTH=1920
 DEAD=2.0**100
 
 def iota(shape,dim): return lax.broadcasted_iota(I32,shape,dim)
@@ -188,32 +217,38 @@
         a=act[f*NB:(f+1)*NB,:].astype(F32)
         d=a-jnp.mean(a,axis=1,keepdims=True)
         v=jnp.mean(d*d,axis=1,keepdims=True)
-        ready=d*lax.rsqrt(v+1e-5)*gain[...]+bias[...]
+        ready=d*lax.rsqrt(v+2*EPS)*gain[...]+bias[...]
         ready=jnp.where(lives>f+0.5,ready,DEAD)
         for j in range(4):
             tall[pl.ds(f*4+j,NB,stride=16),:]=ready[:,j*128:(j+1)*128]
     for b in range(NB):
         send[b]=tall[b*16:(b+1)*16,:].astype(BF)
 
-def unpack_frames(recv,order,tall,out):
+def unpack_frames(recv,order,tall,proj,proj_bias,out):
     for s in range(SHARDS):
         tall[s*16:(s+1)*16,:]=recv[s].astype(F32)
     a=jnp.concatenate([tall[pl.ds(j,128,stride=4),:] for j in range(4)],axis=1).astype(BF)
-    out[...]=jnp.dot(order,a,preferred_element_type=F32).astype(BF)
+    ready=jnp.dot(order,a,preferred_element_type=F32)
+    dead=ready[:,0:1]>DEAD/2
+    ready=ready.astype(BF)
+    for j in range(0,WIDTH,384):
+        p=jnp.dot(ready,proj[:,j:j+384],preferred_element_type=F32)+proj_bias[:,j:j+384]
+        out[:,j:j+384]=jnp.where(dead,0.0,p).astype(BF)
 
 def center_all(ref,depth):
     for l in range(ref.shape[0]):
         def b(i,_):
-            r=pl.ds(pl.multiple_of(i*128,128),128)
+            r=pl.ds(pl.multiple_of(i*512,512),512)
             ref[l,r,:]=center(ref[l,r,:]).astype(BF); return 0
-        lax.fori_loop(0,depth//128,b,0)
-
-def mega(wave,packing,live,placing,w0,wm_h,wl_h,gain,bias,out,
+        lax.fori_loop(0,depth//512,b,0)
+
+def mega(wave,packing,live,placing,w0,wm_h,wl_h,gain,bias,proj_h,proj_bias,out,
          xf,w0s,wm,wl,lhs,*rest):
-    acts=rest[:7]
-    hA,hB,xa,tall,tall2,send1,recv1,send2,recv2,wsem,s1,r1,s2,r2=rest[7:]
+    acts=rest[:8]
+    hA,hB,gA,gB,proj,xa,tall,tall2,send1,recv1,send2,recv2,wsem,s1,r1,s2,r2=rest[8:]
     cps=[pltpu.make_async_copy(wm_h.at[l],wm.at[l],wsem.at[l]) for l in range(4)]
     cps+=[pltpu.make_async_copy(wl_h.at[l],wl.at[l],wsem.at[4+l]) for l in range(2)]
+    cps+=[pltpu.make_async_copy(proj_h,proj,wsem.at[6])]
     for c in cps: c.start()
     barrier=greet()
     pack_waves(wave,packing,live,xa,tall,send1)
@@ -234,9 +269,9 @@
         wave_copy(k,send1,recv1,s1,r1).wait(); return 0
     lax.fori_loop(1,ROWS,done,0)
     unpack_waves(recv1,order,tall,xa,xf)
-    extract(xf,w0s,wm,wl,lhs,acts,hA,hB)
+    extract(xf,w0s,wm,wl,lhs,acts,hA,hB,gA,gB)
     lives=jnp.sum(jnp.where(iota((NB,128),1)==SAMPLES-1280,xf[:,1280:1408],0.0),axis=1,keepdims=True)
-    pack_frames(acts[6],lives,gain,bias,tall2,send2)
+    pack_frames(acts[7],lives,gain,bias,tall2,send2)
     def go2(k,_):
         frame_copy(k,send2,recv2,s2,r2).start(); return 0
     lax.fori_loop(1,SHARDS,go2,0)
@@ -245,20 +280,20 @@
     def done2(k,_):
         frame_copy(k,send2,recv2,s2,r2).wait(); return 0
     lax.fori_loop(1,SHARDS,done2,0)
-    unpack_frames(recv2,forder,tall2,out)
-
-def call_mega(wave,packing,live,placing,w0,wm,wl,g,b):
+    unpack_frames(recv2,forder,tall2,proj,proj_bias,out)
+
+def call_mega(wave,packing,live,placing,w0,wm,wl,g,b,proj,proj_bias):
     V=pl.BlockSpec(memory_space=pltpu.VMEM); A=pl.BlockSpec(memory_space=pl.ANY)
     D=pltpu.SemaphoreType.DMA
-    return pl.pallas_call(mega,out_shape=jax.ShapeDtypeStruct((128,C),BF),
-     in_specs=[V,V,V,V,V,A,A,V,V],out_specs=V,
+    return pl.pallas_call(mega,out_shape=jax.ShapeDtypeStruct((128,WIDTH),BF),
+     in_specs=[V,V,V,V,V,A,A,V,V,A,V],out_specs=V,
      scratch_shapes=[pltpu.VMEM((32,1536),F32),pltpu.VMEM((256,C),BF),pltpu.VMEM((4,1536,C),BF),pltpu.VMEM((2,1024,C),BF),
-       pltpu.VMEM((272*32,128),BF)]+act_scratch()+[pltpu.VMEM((MAXM,C),F32)]*2+[
+       pltpu.VMEM((272*32,128),BF)]+act_scratch()+[pltpu.VMEM((HM,C),F32)]*2+[pltpu.VMEM((GM,C),F32)]*2+[pltpu.VMEM((C,WIDTH),BF),
        pltpu.VMEM((NB,1408),BF),pltpu.VMEM((ROWS*SLAB,128),F32),pltpu.VMEM((SHARDS*16,128),F32),
        pltpu.VMEM((ROWS,SLAB,128),BF),pltpu.VMEM((ROWS,SLAB,128),BF),pltpu.VMEM((SHARDS,16,128),BF),pltpu.VMEM((SHARDS,16,128),BF),
-       D((6,)),D((ROWS,)),D((ROWS,)),D((SHARDS,)),D((SHARDS,))],
+       D((7,)),D((ROWS,)),D((ROWS,)),D((SHARDS,)),D((SHARDS,))],
      compiler_params=pltpu.CompilerParams(vmem_limit_bytes=60*2**20,collective_id=0,has_side_effects=True),name="extract")(
-       wave,packing,live,placing,w0,wm,wl,g,b)
+       wave,packing,live,placing,w0,wm,wl,g,b,proj,proj_bias)
 
 
 def body(
@@ -274,7 +309,7 @@
     projection,
     projection_bias,
 ):
-    arrived = call_mega(
+    encoded = call_mega(
         waveform[0],
         packing,
         live_frames,
@@ -284,12 +319,10 @@
         last_kernels,
         norm_gain.reshape(1, C),
         norm_bias.reshape(1, C),
+        projection,
+        projection_bias.reshape(1, WIDTH),
     )
-    projected = (
-        jnp.dot(arrived, projection, preferred_element_type=F32) + projection_bias
-    )
-    dead = arrived[:, :1] > DEAD / 2
-    return jnp.where(dead, 0.0, projected).astype(BF)[None]
+    return encoded[None]
 
 
 def solution(mesh):

time: 50.6 us -> 47.2 us (0.933)
  Pallas kernels: 47.3 us -> 43.9 us
  local copies, waits for them, and re-layouts: 0.01 us -> 3.14 us
  matrix products: 2.15 us -> 0 us
  other arithmetic: 0.86 us -> 0 us
    pallas_call x1, Pallas kernels: 47.3 us -> 43.9 us  [call_mega(): pl.pallas_call(mega, out_shape=jax.ShapeDtypeStruct((128, WIDTH), BF), in...]
    dot_general x1 -> x0, matrix products: 2.15 us -> none  [body(): jnp.dot(arrived, projection, preferred_element_type=F32) + projection_bias]
    unnamed x4 -> x1, local copies, waits for them, and re-layouts: 0.01 us -> 1.84 us
    reshape x0 -> x1, local copies, waits for them, and re-layouts: none -> 1.3 us  [body(): projection_bias.reshape(1, WIDTH)]
    gt x1 -> x0, other arithmetic: 0.86 us -> none  [body(): dead = arrived[:, :1] > DEAD / 2]
where the time goes in v2:
time: 47.2 us; the launch traced here: 47 us
  Pallas kernels  43.9 us (93%)
  local copies, waits for them, and re-layouts  3.14 us (7%)
    pallas_call x1, Pallas kernels, call_mega(): pl.pallas_call(mega, out_shape=jax.ShapeDtypeStruct((128, WIDTH), BF), in...  43.9 us
    unnamed x1, local copies, waits for them, and re-layouts  1.84 us
    reshape x1, local copies, waits for them, and re-layouts, body(): projection_bias.reshape(1, WIDTH)  1.3 us

profile of v2, /device:TPU:1, one launch (start us, length us, event | category | flops | bytes accessed | tf_op | source)
XLA Modules:
  0.0 47.0 jit_solution(2123652614659975153)
XLA Ops:
  0.0 1.3 %reshape.15.proj_bias = f32[1,1920]{1,0:T(1,128)} reshape(f32[1920]{0:T(1024)} %param.21) | data formatting | bytes 15360 | tf_op jit(solution)/shard_map/reshape | solution.py:323
  1.3 43.9 %extract.1 = bf16[128,1920]{1,0:T(8,128)(2,1)} custom-call(bf16[32,1360]{1,0:T(8,128)(2,1)} %bitcast.6, s32[8,32]{1,0:T(8,128)} %packing.1, s32[1,32]{1,0:T(1,128)} %live.1, s32[8,128]{1,0:T(8,128)} %bitcast.7, bf16[10,512]{1,0:T(8,128)(2,1)} %w0.1, bf16[4,1536,512]{2,1,0:T(8,128)(2,1)} %wm_h.1, bf16[2,1024,512]{2,1,0:T(8,128)(2,1)} %wl_h.1, ...), custom_call_target="tpu_custom_call" | custom-call | tf_op jit(solution)/shard_map/extract/pallas_call | solution.py:288
  45.2 1.8 %copy.13 = bf16[1,128,1920]{2,1,0:T(8,128)(2,1)} copy(bf16[1,128,1920]{2,1,0:T(8,128)(2,1)} %bitcast.5) | data formatting | bytes 983040

commit v3 on v2

--- a/solution.py
+++ b/solution.py
@@ -15,7 +15,7 @@
     w=w.astype(F32)
     return w-jnp.mean(w,axis=1,keepdims=True)
 
-F1=8
+F1=34
 EPS=1e-05
 PLAN={0:(272,16),1:(136,8),2:(67,17),3:(33,11),4:(16,8),5:(8,8),6:(4,4)}
 def nchunk(l): return -(-PLAN[l][0]//PLAN[l][1])
@@ -38,8 +38,8 @@
     else:
         el(n-1,hA)
 
-def build_lhs(xf,lhs):
-    for t in range(272):
+def build_lhs(xf,lhs,first,last):
+    for t in range(first,last):
         o=5*t; j=o//128*128; o-=j
         if o<=118:
             v=xf[:,j:j+128]
@@ -48,10 +48,10 @@
             v=pltpu.roll(xf[:,j:j+256],256-o,1)[:,:128]
         lhs[t*NB:(t+1)*NB,:]=v.astype(BF)
 
-def first_two(lhs,w0,w1,pair,act1,hs,gs):
+def first_two(xf,lhs,w0,w1,pair,act1,hs,gs):
     n=136//F1; M1=F1*NB; M0=2*M1; E=2*NB
     def mm0(i,h):
-        a=lhs[pl.ds(pl.multiple_of(i*M0,M0),M0),:]
+        a=lhs[i*M0:(i+1)*M0,:]
         h[0:M0,:]=jnp.dot(jnp.concatenate([a,a],axis=1),w0[...],preferred_element_type=F32)
     def mm1(g,src):
         v=src.reshape(F1+1,2*NB,C)
@@ -64,28 +64,22 @@
             out[E+r:E+r+RG,:]=v
             if r>=M0-E: nxt[r-(M0-E):r-(M0-E)+RG,:]=v
     def el1(i,g):
-        base=pl.multiple_of(i*M1,M1)
-        for r in range(0,M1,RG):
-            act1[pl.ds(base+r,RG),:]=act_rows(g[r:r+RG,:],2*EPS)
+        for r in range(i*M1,(i+1)*M1,RG):
+            act1[r:r+RG,:]=act_rows(g[r-i*M1:r-i*M1+RG,:],2*EPS)
     def step(i,par,m0=True,e0=True,m1=True,e1=True):
+        if i+2<n: build_lhs(xf,lhs,(i+2)*2*F1,(i+3)*2*F1)
         if m0: mm0(i+1,hs[1-par])
         if m1: mm1(gs[1-par],pair[1-par])
         if e0: el0(hs[par],pair[par],pair[1-par])
         if e1: el1(i-2,gs[par])
+    def edge(i):
+        step(i,i%2,m0=i+1<n,e0=i<n,m1=0<=i-1<n,e1=0<=i-2<n)
+    build_lhs(xf,lhs,0,4*F1)
     mm0(0,hs[0])
-    step(0,0,m1=False,e1=False)
-    step(1,1,e1=False)
-    pairs=(n-3)//2
-    def body(j,_):
-        step(2+2*j,0); step(3+2*j,1)
-        return 0
-    lax.fori_loop(0,pairs,body,0)
-    for i in range(2+2*pairs,n+2):
-        step(i,i%2,m0=i+1<n,e0=i<n,m1=0<=i-1<n,e1=0<=i-2<n)
+    for i in range(n+2): edge(i)
 
 def extract(xf,w0,wm,wl,lhs,acts,hA,hB,gA,gB):
-    build_lhs(xf,lhs)
-    first_two(lhs,w0,wm.at[0],acts[0:2],acts[2],(hA,hB),(gA,gB))
+    first_two(xf,lhs,w0,wm.at[0],acts[0:2],acts[2],(hA,hB),(gA,gB))
     for l in range(2,7):
         T,Tc=PLAN[l]; M=Tc*NB; n=nchunk(l)
         out=acts[l+1]
@@ -235,8 +229,9 @@
         p=jnp.dot(ready,proj[:,j:j+384],preferred_element_type=F32)+proj_bias[:,j:j+384]
         out[:,j:j+384]=jnp.where(dead,0.0,p).astype(BF)
 
-def center_all(ref,depth):
+def center_all(ref,depth,copies):
     for l in range(ref.shape[0]):
+        copies[l].wait()
         def b(i,_):
             r=pl.ds(pl.multiple_of(i*512,512),512)
             ref[l,r,:]=center(ref[l,r,:]).astype(BF); return 0
@@ -263,8 +258,7 @@
     wc=center(w0[...]); hi=wc.astype(BF)
     w0s[...]=jnp.zeros((256,C),BF)
     w0s[0:10,:]=hi; w0s[128:138,:]=(wc-hi.astype(F32)).astype(BF)
-    for c in cps: c.wait()
-    center_all(wm,1536); center_all(wl,1024)
+    center_all(wm,1536,cps[0:4]); center_all(wl,1024,cps[4:6])
     def done(k,_):
         wave_copy(k,send1,recv1,s1,r1).wait(); return 0
     lax.fori_loop(1,ROWS,done,0)
@@ -280,12 +274,13 @@
     def done2(k,_):
         frame_copy(k,send2,recv2,s2,r2).wait(); return 0
     lax.fori_loop(1,SHARDS,done2,0)
+    cps[6].wait()
     unpack_frames(recv2,forder,tall2,proj,proj_bias,out)
 
 def call_mega(wave,packing,live,placing,w0,wm,wl,g,b,proj,proj_bias):
     V=pl.BlockSpec(memory_space=pltpu.VMEM); A=pl.BlockSpec(memory_space=pl.ANY)
     D=pltpu.SemaphoreType.DMA
-    return pl.pallas_call(mega,out_shape=jax.ShapeDtypeStruct((128,WIDTH),BF),
+    return pl.pallas_call(mega,out_shape=pltpu.VMEM((128,WIDTH),BF),
      in_specs=[V,V,V,V,V,A,A,V,V,A,V],out_specs=V,
      scratch_shapes=[pltpu.VMEM((32,1536),F32),pltpu.VMEM((256,C),BF),pltpu.VMEM((4,1536,C),BF),pltpu.VMEM((2,1024,C),BF),
        pltpu.VMEM((272*32,128),BF)]+act_scratch()+[pltpu.VMEM((HM,C),F32)]*2+[pltpu.VMEM((GM,C),F32)]*2+[pltpu.VMEM((C,WIDTH),BF),

time: 47.2 us -> 43.1 us (0.913)
  Pallas kernels: 43.9 us -> 40.9 us
  local copies, waits for them, and re-layouts: 3.14 us -> 2.08 us
    pallas_call x1, Pallas kernels: 43.9 us -> 40.9 us  [call_mega(): pl.pallas_call(mega, out_shape=pltpu.VMEM((128, WIDTH), BF), in_specs=[V,...]
    unnamed x1, local copies, waits for them, and re-layouts: 1.84 us -> 0.78 us
where the time goes in v3:
time: 43.1 us; the launch traced here: 43 us
  Pallas kernels  40.9 us (95%)
  local copies, waits for them, and re-layouts  2.08 us (5%)
    pallas_call x1, Pallas kernels, call_mega(): pl.pallas_call(mega, out_shape=pltpu.VMEM((128, WIDTH), BF), in_specs=[V,...  40.9 us
    reshape x1, local copies, waits for them, and re-layouts, body(): projection_bias.reshape(1, WIDTH)  1.3 us

profile of v3, /device:TPU:1, one launch (start us, length us, event | category | flops | bytes accessed | tf_op | source)
XLA Modules:
  0.0 43.0 jit_solution(18226875537808658258)
XLA Ops:
  0.0 1.3 %reshape.15.proj_bias = f32[1,1920]{1,0:T(1,128)} reshape(f32[1920]{0:T(1024)} %param.21) | data formatting | bytes 15360 | tf_op jit(solution)/shard_map/reshape | solution.py:318
  1.3 40.9 %extract.1 = bf16[128,1920]{1,0:T(8,128)(2,1)S(1)} custom-call(bf16[32,1360]{1,0:T(8,128)(2,1)} %bitcast.6, s32[8,32]{1,0:T(8,128)} %packing.1, s32[1,32]{1,0:T(1,128)} %live.1, s32[8,128]{1,0:T(8,128)} %bitcast.7, bf16[10,512]{1,0:T(8,128)(2,1)} %w0.1, bf16[4,1536,512]{2,1,0:T(8,128)(2,1)} %wm_h.1, bf16[2,1024,512]{2,1,0:T(8,128)(2,1)} %wl_h.1, ...), custom_call_target="tpu_custom_call" | custom-call | tf_op jit(solution)/shard_map/extract/pallas_call | solution.py:283
  42.2 0.8 %copy.13 = bf16[1,128,1920]{2,1,0:T(8,128)(2,1)} copy(bf16[1,128,1920]{2,1,0:T(8,128)(2,1)S(1)} %bitcast.5) | data formatting | bytes 983040

commit v4 on v3

--- a/solution.py
+++ b/solution.py
@@ -118,6 +118,8 @@
 SAMPLES=1360
 WIDTH=1920
 DEAD=2.0**100
+def hops(k): return min(k//8,4-k//8)+min(k%8,8-k%8)
+FAR_FIRST=sorted(range(1,SHARDS),key=lambda k:-hops(k))
 
 def iota(shape,dim): return lax.broadcasted_iota(I32,shape,dim)
 def earlier_counts(owned):
@@ -127,7 +129,8 @@
 def dp_peer(k):
     return lax.rem(lax.axis_index("dp")+k,ROWS)
 def seq_peer(k):
-    return lax.rem(lax.axis_index("seq")+k,SHARDS)
+    me=lax.axis_index("seq")
+    return lax.rem(me//8+k//8,4)*8+lax.rem(lax.rem(me,8)+k%8,8)
 def row_of_shard(s):
     return lax.rem(s,4)*8+s//4
 
@@ -266,9 +269,7 @@
     extract(xf,w0s,wm,wl,lhs,acts,hA,hB,gA,gB)
     lives=jnp.sum(jnp.where(iota((NB,128),1)==SAMPLES-1280,xf[:,1280:1408],0.0),axis=1,keepdims=True)
     pack_frames(acts[7],lives,gain,bias,tall2,send2)
-    def go2(k,_):
-        frame_copy(k,send2,recv2,s2,r2).start(); return 0
-    lax.fori_loop(1,SHARDS,go2,0)
+    for k in FAR_FIRST: frame_copy(k,send2,recv2,s2,r2).start()
     ms=lax.axis_index("seq")
     recv2[ms]=send2[row_of_shard(ms)]
     def done2(k,_):

time: 43.1 us -> 43.2 us (level)
  no operation moved by 1% of the time
where the time goes in v4:
time: 43.2 us; the launch traced here: 43 us
  Pallas kernels  40.9 us (95%)
  local copies, waits for them, and re-layouts  2.08 us (5%)
    pallas_call x1, Pallas kernels, call_mega(): pl.pallas_call(mega, out_shape=pltpu.VMEM((128, WIDTH), BF), in_specs=[V,...  40.9 us
    reshape x1, local copies, waits for them, and re-layouts, body(): projection_bias.reshape(1, WIDTH)  1.3 us

profile of v4, /device:TPU:1, one launch (start us, length us, event | category | flops | bytes accessed | tf_op | source)
XLA Modules:
  0.0 43.0 jit_solution(18410984620800946594)
XLA Ops:
  0.0 1.3 %reshape.15.proj_bias = f32[1,1920]{1,0:T(1,128)} reshape(f32[1920]{0:T(1024)} %param.21) | data formatting | bytes 15360 | tf_op jit(solution)/shard_map/reshape | solution.py:319
  1.3 40.9 %extract.1 = bf16[128,1920]{1,0:T(8,128)(2,1)S(1)} custom-call(bf16[32,1360]{1,0:T(8,128)(2,1)} %bitcast.6, s32[8,32]{1,0:T(8,128)} %packing.1, s32[1,32]{1,0:T(1,128)} %live.1, s32[8,128]{1,0:T(8,128)} %bitcast.7, bf16[10,512]{1,0:T(8,128)(2,1)} %w0.1, bf16[4,1536,512]{2,1,0:T(8,128)(2,1)} %wm_h.1, bf16[2,1024,512]{2,1,0:T(8,128)(2,1)} %wl_h.1, ...), custom_call_target="tpu_custom_call" | custom-call | tf_op jit(solution)/shard_map/extract/pallas_call | solution.py:284
  42.2 0.8 %copy.13 = bf16[1,128,1920]{2,1,0:T(8,128)(2,1)} copy(bf16[1,128,1920]{2,1,0:T(8,128)(2,1)S(1)} %bitcast.5) | data formatting | bytes 983040
